TPU v7x, 32 devices: a whole 2x2x4 slice. The times are simulated.
32 devices in a mesh: dp: 4 (over x, core), tensor: 8 (over z, y).
Axes of the slice: x: 2, y: 2, z: 4, core: 2. Of those that a mesh axis runs over, the one named last changes fastest.
Arguments:
- train_acts: bfloat16 [256, 64, 28672], P('dp', None, 'tensor'), may hold values from -6 to 6
- train_grads: bfloat16 [256, 64, 8192], P('dp', None, 'tensor'), may hold values from -6 to 6
- query_acts: bfloat16 [64, 64, 28672], P('dp', None, 'tensor'), may hold values from -6 to 6
- query_grads: bfloat16 [64, 64, 8192], P('dp', None, 'tensor'), may hold values from -6 to 6
- proj_in: bfloat16 [28672, 32], P('tensor'), may hold values from -0.03125 to 0.03125
- proj_out: bfloat16 [8192, 32], P('tensor'), may hold values from -0.0625 to 0.0625
- train_counts: int32 [256], P('dp'), may hold values from 16 to 64
- query_counts: int32 [64], P('dp'), may hold values from 16 to 64
Outputs:
- scores: float32 [64, 256], P('tensor', 'dp')
All inputs are finite; a program needn't handle non-finite values.
Results may differ from a plain program's by a relative error of at most 0.0003.
Values sent between devices are 32-bit elements; how exact they have to be, the bound alone decides.
A program may use at most 192 MiB of HBM per device.

v0:
```python
import functools

import jax
import jax.numpy as jnp
from jax import lax
from jax.experimental import pallas as pl
from jax.experimental.pallas import tpu as pltpu
from jax.sharding import PartitionSpec as P

LANES = 128


def project_pair(acts, grads, proj_in, proj_out):
    xproj = jnp.einsum("stf,fr->srt", acts, proj_in, preferred_element_type=jnp.float32)
    gproj = jnp.einsum("std,dr->srt", grads, proj_out, preferred_element_type=jnp.float32)
    joined = jnp.concatenate([gproj, xproj], axis=1)
    return joined.reshape(joined.shape[0], -1)


def form_sketches(joined, counts, width, length):
    joined = joined.reshape(joined.shape[0], 2 * width, length)
    valid = (jnp.arange(length, dtype=jnp.int32)[None, :] < counts[:, None]).astype(jnp.float32)
    gproj = joined[:, :width, :] * valid[:, None, :]
    xproj = joined[:, width:, :]
    block = jnp.einsum(
        "sat,sbt->sab",
        gproj,
        xproj,
        precision=lax.Precision.HIGHEST,
        preferred_element_type=jnp.float32,
    )
    return block.reshape(block.shape[0], width * width)


def bcast_row(tile, i):
    return jnp.broadcast_to(tile[i : i + 1, :], tile.shape)


def lane_pick(tile, index):
    return jnp.take_along_axis(tile, index, axis=1, mode="promise_in_bounds")


def solve_kernel(rows_out, scale, s_ref, q_ref, cnt_ref, out_ref, wide, qwide, a_ref):
    n = a_ref.shape[0]
    nq = qwide.shape[0]
    parts = s_ref.shape[0] // n
    tiles = n // LANES
    dims = (((1,), (1,)), ((), ()))
    exact = dict(precision=lax.Precision.HIGHEST, preferred_element_type=jnp.float32)
    for r in range(parts):
        wide[:, r * LANES : (r + 1) * LANES] = s_ref[pl.ds(r, n, stride=parts), :]
        qwide[:, r * LANES : (r + 1) * LANES] = q_ref[pl.ds(r, nq, stride=parts), :]
    total = jnp.sum(cnt_ref[...])
    gram = lax.dot_general(wide[...], wide[...], dims, **exact)
    cross = lax.dot_general(qwide[...], wide[...], dims, **exact)
    diag = lax.broadcasted_iota(jnp.int32, (n, n), 0) == lax.broadcasted_iota(jnp.int32, (n, n), 1)
    lam = 0.1 * (jnp.sum(jnp.where(diag, gram, 0.0)) / total) / (parts * LANES)
    a_ref[...] = gram / total + jnp.where(diag, lam, 0.0)

    sub = lax.broadcasted_iota(jnp.int32, (8, LANES), 0)
    lane = lax.broadcasted_iota(jnp.int32, (8, LANES), 1)

    def block(kb, carry):
        k0 = pl.multiple_of(kb * 8, 8)
        kt = pl.multiple_of((k0 // LANES) * LANES, LANES)
        kl = k0 % LANES
        picks = [jnp.full((8, LANES), kl + i, jnp.int32) for i in range(8)]
        pivot = a_ref[pl.ds(k0, 8), pl.ds(kt, LANES)]
        cols = [lane_pick(pivot, picks[i]) for i in range(8)]
        inside, right = [], []
        for j in range(tiles):
            offset = lane + (j * LANES - k0)
            mask = (offset >= 0) & (offset < 8)
            inside.append(mask)
            row = a_ref[pl.ds(k0, 8), j * LANES : (j + 1) * LANES]
            right.append(jnp.where(mask, jnp.where(offset == sub, 1.0, 0.0), row))
        for i in range(8):
            own = sub == i
            inv = 1.0 / bcast_row(cols[i], i)
            factor = cols[i]
            for m in range(i + 1, 8):
                row = bcast_row(cols[m], i) * inv
                cols[m] = jnp.where(own, row, cols[m] - factor * row)
            for j in range(tiles):
                row = bcast_row(right[j], i) * inv
                right[j] = jnp.where(own, row, right[j] - factor * row)
        spread = [[bcast_row(right[j], i) for j in range(tiles)] for i in range(8)]
        for rt in range(n // 8):
            here = slice(rt * 8, rt * 8 + 8)
            column = a_ref[here, pl.ds(kt, LANES)]
            heads = [lane_pick(column, picks[i]) for i in range(8)]
            for j in range(tiles):
                there = slice(j * LANES, (j + 1) * LANES)
                value = jnp.where(inside[j], 0.0, a_ref[here, there])
                for i in range(8):
                    value = value - heads[i] * spread[i][j]
                a_ref[here, there] = value
        for j in range(tiles):
            a_ref[pl.ds(k0, 8), j * LANES : (j + 1) * LANES] = right[j]
        return carry

    lax.fori_loop(0, n // 8, block, 0)
    first = pl.multiple_of(lax.axis_index("dp") * rows_out, 8)
    out_ref[...] = lax.dot_general(cross, a_ref[pl.ds(first, rows_out), :], dims, **exact) / scale


def solve(train, query, counts, n, nq, rows_out):
    width = train.shape[0] * LANES // n
    return pl.pallas_call(
        functools.partial(solve_kernel, rows_out, n),
        out_shape=jax.ShapeDtypeStruct((nq, rows_out), jnp.float32),
        in_specs=[pl.BlockSpec(memory_space=pltpu.VMEM)] * 3,
        out_specs=pl.BlockSpec(memory_space=pltpu.VMEM),
        scratch_shapes=[
            pltpu.VMEM((n, width), jnp.float32),
            pltpu.VMEM((nq, width), jnp.float32),
            pltpu.VMEM((n, n), jnp.float32),
        ],
        compiler_params=pltpu.CompilerParams(vmem_limit_bytes=48 * 2**20),
    )(train, query, counts)


def local(
    train_acts, train_grads, query_acts, query_grads, proj_in, proj_out, train_counts, query_counts
):
    width = proj_in.shape[1]
    length = train_acts.shape[1]
    train_pair = project_pair(train_acts, train_grads, proj_in, proj_out)
    query_pair = lax.psum(project_pair(query_acts, query_grads, proj_in, proj_out), "tensor")
    query_sketch = form_sketches(query_pair, query_counts, width, length)
    every_query = lax.all_gather(query_sketch, "dp", axis=0, tiled=True)
    full_pair = lax.psum(train_pair, "tensor")
    local_train = form_sketches(full_pair, train_counts, width, length)
    every_train, every_count = (
        lax.all_gather(local_train, "dp", axis=0, tiled=True),
        lax.all_gather(train_counts, "dp", axis=0, tiled=True),
    )
    query_share = every_query.shape[0] // lax.axis_size("tensor")
    my_queries = lax.dynamic_slice_in_dim(
        every_query, lax.axis_index("tensor") * query_share, query_share
    )
    n = every_train.shape[0]
    return solve(
        every_train.reshape(-1, LANES),
        my_queries.reshape(-1, LANES),
        every_count.astype(jnp.float32).reshape(-1, LANES),
        n,
        query_share,
        local_train.shape[0],
    )


def solution(mesh):
    placed = (
        P("dp", None, "tensor"),
        P("dp", None, "tensor"),
        P("dp", None, "tensor"),
        P("dp", None, "tensor"),
        P("tensor", None),
        P("tensor", None),
        P("dp"),
        P("dp"),
    )
    return jax.shard_map(
        local, mesh=mesh, in_specs=placed, out_specs=P("tensor", "dp"), check_vma=False
    )
```

profile of v0, /device:TPU:0, one launch (start us, length us, event | category | flops | bytes accessed | tf_op | source)
XLA Modules:
  0.0 294.5 jit_solution(1650653376472505688)
XLA Ops:
  6.5 0.0 copy-start
  6.5 0.0 copy-start.1
  6.5 0.0 all-reduce.4.cloned.1.call-start
  6.5 22.6 %convolution_bitcast_fusion = f32[64,32,64]{2,1,0:T(8,128)S(1)} fusion(bf16[64,64,3584]{2,1,0:T(8,128)(2,1)} %param.8, bf16[3584,32]{0,1:T(8,128)(2,1)} %param.12), kind=kOutput, calls=%fused_computation.1 | convolution fusion | flops 939524096 | bytes 30113792 | tf_op jit(solution)/shard_map/stf,fr->srt/dot_general | solution.py:14
  29.1 0.0 copy-done.1
  29.2 0.0 copy-start.2
  29.2 6.5 %convolution_bitcast_fusion.3 = f32[16,32,64]{2,1,0:T(8,128)S(1)} fusion(bf16[16,64,3584]{2,1,0:T(8,128)(2,1)} %param.10, bf16[3584,32]{0,1:T(8,128)(2,1)S(1)} %copy-done.1), kind=kOutput, calls=%fused_computation.4 | convolution fusion | flops 234881024 | bytes 7700480 | tf_op jit(solution)/shard_map/stf,fr->srt/dot_general | solution.py:14
  35.7 0.0 copy-done.2
  35.7 7.3 %convolution_bitcast_fusion.1 = f32[64,32,64]{2,1,0:T(8,128)S(1)} fusion(bf16[64,64,1024]{2,1,0:T(8,128)(2,1)} %param.9, bf16[1024,32]{0,1:T(8,128)(2,1)S(1)} %copy-done.2), kind=kOutput, calls=%fused_computation.2 | convolution fusion | flops 268435456 | bytes 8978432 | tf_op jit(solution)/shard_map/std,dr->srt/dot_general | solution.py:15
  43.0 0.0 copy-done
  43.1 0.0 copy-start.3
  43.1 1.1 convolution_bitcast_fusion.2
  44.1 0.0 copy-start.5
  44.2 0.0 copy-start.4
  44.2 1.5 pad_maximum_fusion
  45.7 0.8 pad_maximum_fusion.1
  46.5 0.0 all-reduce.4.cloned.1.call-update
  46.5 0.0 all-gather.2.cloned.1.call-start
  46.6 0.0 copy-done.3
  46.6 0.1 fusion.10
  46.7 118.9 %all-reduce.4.cloned.1.call-done = (f32[64,64,64]{2,1,0:T(8,128)}, f32[16,64,64]{2,1,0:T(8,128)}) async-done(((f32[64,64,64]{2,1,0:T(8,128)}, f32[16,64,64]{2,1,0:T(8,128)}), (f32[64,64,64]{2,1,0:T(8,128)}, f32[16,64,64]{2,1,0:T(8,128)})) %all-reduce.4.cloned.1.call-update) | async-done | bytes 1310736 | tf_op jit(solution)/shard_map/psum | solution.py:132
  165.5 3.4 %fusion = f32[64,32,32]{2,1,0:T(8,128)S(1)} fusion(f32[64,64,64]{2,1,0:T(8,128)} %get-tuple-element.5, f32[64,64]{1,0:T(8,128)S(1)} %fusion.10), kind=kOutput, calls=%fused_computation.5 | convolution fusion | flops 50462720 | bytes 1327104 | tf_op jit(solution)/shard_map/sat,sbt->sab/dot_general | solution.py:25
  168.9 1.4 copy.11
  170.3 1.9 copy.12
  172.2 0.0 all-gather.2.cloned.1.call-update
  172.3 0.0 copy-done.5
  172.3 0.6 dynamic-slice
  173.5 0.2 dynamic-update-slice
  173.8 4.9 %all-reduce = s32[256]{0:T(256)S(1)} all-reduce(s32[256]{0:T(256)S(1)} %dynamic-update-slice), channel_id=1, replica_groups=mesh['dp'=4,'tensor'=8] {'dp'}, use_global_device_ids=true, to_apply=%add | all-reduce | flops 256 | bytes 2048
  178.7 0.0 copy-done.4
  178.7 0.1 fusion.11
  178.7 1.6 fusion.3
  180.3 0.1 reshape.69
  180.5 7.6 %all_gather.10 = f32[64,1024]{1,0:T(8,128)S(1)} all-gather(f32[16,1024]{1,0:T(8,128)S(1)} %reshape.69), channel_id=1, replica_groups=mesh['dp'=4,'tensor'=8] {'dp'}, dimensions={0}, use_global_device_ids=true | all-gather | bytes 327680 | tf_op jit(solution)/shard_map/all_gather | solution.py:131
  188.1 1.5 all-gather.2.cloned.1.call-done
  189.6 1.4 reshape.66.s_ref
  191.0 96.7 %shard_map.82 = f32[8,64]{1,0:T(8,128)} custom-call(f32[2048,128]{1,0:T(8,128)S(1)} %reshape.66.s_ref, f32[64,128]{1,0:T(8,128)S(1)} %reshape.70.q_ref, f32[2,128]{1,0:T(2,128)S(1)} %convert_bitcast_fusion.cnt_ref), custom_call_target="tpu_custom_call" | custom-call | tf_op jit(solution)/shard_map/pallas_call | solution.py:109
  (4 shorter events, 0.0 us)
Async XLA Ops:
  6.5 36.5 %copy-start = (bf16[16,64,1024]{2,1,0:T(8,128)(2,1)S(1)}, bf16[16,64,1024]{2,1,0:T(8,128)(2,1)}, u32[]{:S(2)}) copy-start(bf16[16,64,1024]{2,1,0:T(8,128)(2,1)} %param.11) | copy-start | bytes 6291460
  6.5 22.6 %copy-start.1 = (bf16[3584,32]{0,1:T(8,128)(2,1)S(1)}, bf16[3584,32]{0,1:T(8,128)(2,1)}, u32[]{:S(2)}) copy-start(bf16[3584,32]{0,1:T(8,128)(2,1)} %param.12) | copy-start | bytes 688132
  6.5 159.0 %all-reduce.4.cloned.1.call-start = ((), (), s32[]{:S(2)}) async-start(), calls=%async_computation.1 | async-start | bytes 5242880 | tf_op jit(solution)/shard_map/psum | solution.py:132
  29.2 6.5 %copy-start.2 = (bf16[1024,32]{0,1:T(8,128)(2,1)S(1)}, bf16[1024,32]{0,1:T(8,128)(2,1)}, u32[]{:S(2)}) copy-start(bf16[1024,32]{0,1:T(8,128)(2,1)} %param.13) | copy-start | bytes 196612
  43.1 3.5 %copy-start.3 = (s32[64]{0:T(128)S(1)}, s32[64]{0:T(128)}, u32[]{:S(2)}) copy-start(s32[64]{0:T(128)} %param.14) | copy-start | bytes 772
  44.1 128.1 %copy-start.5 = (u32[32]{0:T(128)S(1)}, u32[32]{0:T(128)}, u32[]{:S(2)}) copy-start(u32[32]{0:T(128)} %constant.12) | copy-start | bytes 388
  44.2 134.5 %copy-start.4 = (s32[16]{0:T(128)S(1)}, s32[16]{0:T(128)}, u32[]{:S(2)}) copy-start(s32[16]{0:T(128)} %param.15) | copy-start | bytes 196
  46.5 143.0 %all-gather.2.cloned.1.call-start = ((), (), s32[]{:S(2)}) async-start(), calls=%async_computation | async-start | bytes 1310720 | tf_op jit(solution)/shard_map/all_gather | solution.py:135
Sparse Core Ops, SparseCore 0:
  46.7 118.8 all-reduce.3
  172.4 17.1 all-gather.1
where the time goes:
time: 295 us; the launch traced here: 294 us
  waiting for transfers between devices  120 us (41%)
  Pallas kernels  96.7 us (33%)
  matrix products  42.4 us (14%)
  between operations  14.2 us (5%)
  blocking collectives  12.5 us (4%)
  local copies, waits for them, and re-layouts  5.77 us (2%)
    psum x1, waiting for transfers between devices, local(): full_pair = lax.psum(train_pair, 'tensor')  119 us
    pallas_call x1, Pallas kernels, solve(): pl.pallas_call(functools.partial(solve_kernel, rows_out, n), out_shape=ja...  96.7 us
    dot_general x2, matrix products, project_pair(): jnp.einsum('stf,fr->srt', acts, proj_in, preferred_element_type=jnp.float32)  29.1 us
    dot_general x2, matrix products, project_pair(): jnp.einsum('std,dr->srt', grads, proj_out, preferred_element_type=jnp.flo...  8.4 us
    all_gather x1, blocking collectives, local(): every_query = lax.all_gather(query_sketch, 'dp', axis=0, tiled=True)  7.58 us
  transfers between devices with their start and end apart: 2, of which 2 were waited for; matrix products, arithmetic and copies ran while one was open for 1% of the time, Pallas kernels for 0%

commit v1 on v0

--- a/solution.py
+++ b/solution.py
@@ -10,26 +10,257 @@
 LANES = 128
 
 
-def project_pair(acts, grads, proj_in, proj_out):
-    xproj = jnp.einsum("stf,fr->srt", acts, proj_in, preferred_element_type=jnp.float32)
-    gproj = jnp.einsum("std,dr->srt", grads, proj_out, preferred_element_type=jnp.float32)
-    joined = jnp.concatenate([gproj, xproj], axis=1)
-    return joined.reshape(joined.shape[0], -1)
-
-
-def form_sketches(joined, counts, width, length):
-    joined = joined.reshape(joined.shape[0], 2 * width, length)
-    valid = (jnp.arange(length, dtype=jnp.int32)[None, :] < counts[:, None]).astype(jnp.float32)
-    gproj = joined[:, :width, :] * valid[:, None, :]
-    xproj = joined[:, width:, :]
-    block = jnp.einsum(
-        "sat,sbt->sab",
-        gproj,
-        xproj,
-        precision=lax.Precision.HIGHEST,
-        preferred_element_type=jnp.float32,
-    )
-    return block.reshape(block.shape[0], width * width)
+def place(width, offset):
+    row = lax.broadcasted_iota(jnp.int32, (width, LANES), 0)
+    col = lax.broadcasted_iota(jnp.int32, (width, LANES), 1)
+    return jnp.where(row + offset == col, 1.0, 0.0).astype(jnp.bfloat16)
+
+
+def sketch_kernel(
+    dps, outer, inner,
+    tacts, tgrads, qacts, qgrads, pin, pout, tcount, qcount,
+    train_out, query_out, count_out,
+    abuf, gbuf, win, wout, yout, yin, own, zin, gath,
+    load_sem, ysend, yrecv, zsend, zrecv, gzs, gzr, gys, gyr, gxs, gxr, gcs, gcr, out_sem,
+):
+    width = pin.shape[1]
+    tensor = outer * inner
+    nt, nq = tacts.shape[0] // tensor, qacts.shape[0] // tensor
+    ns = nt + nq
+    half = tacts.shape[1] // 2
+    feat, model = pin.shape[0], pout.shape[0]
+    chips = dps // 2
+    dp, me = lax.axis_index("dp"), lax.axis_index("tensor")
+    z, y = me // inner, me % inner
+    x, core = dp // 2, dp % 2
+    mesh_id = pl.DeviceIdType.MESH
+
+    def at_z(k):
+        return (dp, ((z + k) % outer) * inner + y)
+
+    def at_y(k):
+        return (dp, z * inner + (y + k) % inner)
+
+    def at_x(k):
+        return (((x + k) % chips) * 2 + core, me)
+
+    sibling = (x * 2 + 1 - core, me)
+
+    steps = [(zi, dy) for zi in range(outer) for dy in list(range(1, inner)) + [0]]
+    slots = abuf.shape[0]
+
+    def loads(step):
+        zi, dy = steps[step]
+        owner = ((z + 1 + zi) % outer) * inner + (y + dy) % inner
+        slot = step % slots
+        pairs = (
+            (tacts.at[pl.ds(owner * nt, nt)], abuf.at[slot, pl.ds(0, nt)]),
+            (tgrads.at[pl.ds(owner * nt, nt)], gbuf.at[slot, pl.ds(0, nt)]),
+            (qacts.at[pl.ds(owner * nq, nq)], abuf.at[slot, pl.ds(nt, nq)]),
+            (qgrads.at[pl.ds(owner * nq, nq)], gbuf.at[slot, pl.ds(nt, nq)]),
+        )
+        return [
+            pltpu.make_async_copy(src, dst, load_sem.at[slot, i])
+            for i, (src, dst) in enumerate(pairs)
+        ]
+
+    for step in range(min(slots, len(steps))):
+        for copy in loads(step):
+            copy.start()
+
+    barrier = pltpu.get_barrier_semaphore()
+    partners = [at_z(k) for k in range(1, outer)] + [at_y(k) for k in range(1, inner)]
+    partners += [at_x(k) for k in range(1, chips)] + [sibling]
+    for partner in partners:
+        pl.semaphore_signal(barrier, inc=1, device_id=partner, device_id_type=mesh_id)
+
+    for h in range(2):
+        win[h] = jnp.dot(
+            pin[...], place(width, 2 * width * h + width), preferred_element_type=jnp.float32
+        ).astype(jnp.bfloat16)
+        wout[h] = jnp.dot(
+            pout[...], place(width, 2 * width * h), preferred_element_type=jnp.float32
+        ).astype(jnp.bfloat16)
+    pl.semaphore_wait(barrier, len(partners))
+
+    def project(slot):
+        total = None
+        for h in range(2):
+            rows = slice(h * half, (h + 1) * half)
+            a = abuf[slot, :, rows, :].reshape(ns * half, feat)
+            g = gbuf[slot, :, rows, :].reshape(ns * half, model)
+            term = jnp.dot(a, win[h], preferred_element_type=jnp.float32)
+            term = term + jnp.dot(g, wout[h], preferred_element_type=jnp.float32)
+            total = term if total is None else total + term
+        return total
+
+    def remote(src, dst, send, recv, target):
+        return pltpu.make_async_remote_copy(
+            src_ref=src, dst_ref=dst, send_sem=send, recv_sem=recv,
+            device_id=target, device_id_type=mesh_id,
+        )
+
+    ycopies, zcopies = {}, []
+
+    def finish(zi):
+        value = own[zi]
+        for dy in range(1, inner):
+            ycopies[zi, dy].wait_recv()
+            value = value + yin[dy - 1, zi]
+        own[zi] = value
+        if zi < outer - 1:
+            copy = remote(
+                own.at[zi], zin.at[zi], zsend.at[zi], zrecv.at[zi], at_z(zi + 1)
+            )
+            copy.start()
+            zcopies.append(copy)
+
+    for step, (zi, dy) in enumerate(steps):
+        for copy in loads(step):
+            copy.wait()
+        value = project(step % slots)
+        if dy:
+            yout[dy - 1, zi] = value
+            copy = remote(
+                yout.at[dy - 1, zi], yin.at[dy - 1, zi],
+                ysend.at[dy - 1, zi], yrecv.at[dy - 1, zi], at_y(dy),
+            )
+            copy.start()
+            ycopies[zi, dy] = copy
+        else:
+            own[zi] = value
+        if step + slots < len(steps):
+            for copy in loads(step + slots):
+                copy.start()
+        if dy == 0 and zi >= 1:
+            finish(zi - 1)
+    finish(outer - 1)
+
+    full = own[outer - 1]
+    for zi, copy in enumerate(zcopies):
+        copy.wait_recv()
+        full = full + zin[zi]
+
+    row = lax.broadcasted_iota(jnp.int32, (half, LANES), 0)
+    col = lax.broadcasted_iota(jnp.int32, (half, LANES), 1)
+    token = row + jnp.where(col >= 2 * width, half, 0)
+    group = lax.broadcasted_iota(jnp.int32, (8, LANES), 1) // width
+    mine = dp * tensor + me
+    count_sum = jnp.int32(0)
+    for s in range(ns):
+        if s < nt:
+            count = tcount[me * nt + s]
+            count_sum = count_sum + count
+        else:
+            count = qcount[me * nq + s - nt]
+        joined = full[s * half : (s + 1) * half]
+        masked = jnp.where(token < count, joined, 0.0)
+        prod = lax.dot_general(
+            masked, joined, (((0,), (0,)), ((), ())),
+            precision=lax.Precision.HIGHEST, preferred_element_type=jnp.float32,
+        )
+        tile = jnp.zeros((8, LANES), jnp.float32)
+        for q in range(width // 8):
+            first = prod[q * 8 : q * 8 + 8]
+            second = prod[2 * width + q * 8 : 2 * width + q * 8 + 8]
+            first = pltpu.roll(first, (q * width - width) % LANES, 1)
+            second = pltpu.roll(second, (q * width - 3 * width) % LANES, 1)
+            tile = jnp.where(group == q, first + second, tile)
+        gath[mine, s * 8 : s * 8 + 8, :] = tile
+    corner = (lax.broadcasted_iota(jnp.int32, (8, LANES), 0) == 0) & (
+        lax.broadcasted_iota(jnp.int32, (8, LANES), 1) == 0
+    )
+    gath[mine, ns * 8 : ns * 8 + 8, :] = jnp.where(corner, count_sum.astype(jnp.float32), 0.0)
+
+    sends = []
+
+    def share(block, send, recv, target):
+        copy = remote(block, block, send, recv, target)
+        copy.start()
+        sends.append(copy)
+        return copy
+
+    zs = [share(gath.at[mine], gzs.at[k - 1], gzr.at[k - 1], at_z(k)) for k in range(1, outer)]
+    ys = []
+    for j in range(outer):
+        if j:
+            zs[j - 1].wait_recv()
+        block = gath.at[dp * tensor + ((z - j + outer) % outer) * inner + y]
+        for k in range(1, inner):
+            ys.append(share(block, gys.at[k - 1, j], gyr.at[k - 1, j], at_y(k)))
+    for copy in ys:
+        copy.wait_recv()
+    block = gath.at[pl.ds(dp * tensor, tensor)]
+    xs = [share(block, gxs.at[k - 1], gxr.at[k - 1], at_x(k)) for k in range(1, chips)]
+    cs = []
+    for j in range(chips):
+        if j:
+            xs[j - 1].wait_recv()
+        block = gath.at[pl.ds((((x - j + chips) % chips) * 2 + core) * tensor, tensor)]
+        cs.append(share(block, gcs.at[j], gcr.at[j], sibling))
+    for copy in cs:
+        copy.wait_recv()
+    finals = [
+        pltpu.make_async_copy(gath.at[:, pl.ds(0, nt * 8)], train_out, out_sem.at[0]),
+        pltpu.make_async_copy(
+            gath.at[pl.ds(me * dps, dps), pl.ds(nt * 8, nq * 8)], query_out, out_sem.at[1]
+        ),
+        pltpu.make_async_copy(gath.at[:, pl.ds(ns * 8, 8)], count_out, out_sem.at[2]),
+    ]
+    for copy in finals:
+        copy.start()
+    for copy in list(ycopies.values()) + zcopies + sends:
+        copy.wait_send()
+    for copy in finals:
+        copy.wait()
+
+
+def sketches(dps, tensor, tacts, tgrads, qacts, qgrads, pin, pout, tcount, qcount):
+    outer = 4 if tensor % 4 == 0 else 1
+    inner = tensor // outer
+    chips = dps // 2
+    nt, nq = tacts.shape[0] // tensor, qacts.shape[0] // tensor
+    ns = nt + nq
+    length, feat, model = tacts.shape[1], tacts.shape[2], tgrads.shape[2]
+    devices = dps * tensor
+    slots = 3
+    f32 = jnp.float32
+    block = (ns * length // 2, LANES)
+    many = lambda *shape: pltpu.SemaphoreType.DMA(tuple(max(1, n) for n in shape))
+    anywhere, vmem = pl.BlockSpec(memory_space=pl.ANY), pl.BlockSpec(memory_space=pltpu.VMEM)
+    smem = pl.BlockSpec(memory_space=pltpu.SMEM)
+    return pl.pallas_call(
+        functools.partial(sketch_kernel, dps, outer, inner),
+        out_shape=(
+            jax.ShapeDtypeStruct((devices, nt * 8, LANES), f32),
+            jax.ShapeDtypeStruct((dps, nq * 8, LANES), f32),
+            jax.ShapeDtypeStruct((devices, 8, LANES), f32),
+        ),
+        in_specs=[anywhere] * 4 + [vmem] * 2 + [smem] * 2,
+        out_specs=(anywhere,) * 3,
+        scratch_shapes=[
+            pltpu.VMEM((slots, ns, length, feat), jnp.bfloat16),
+            pltpu.VMEM((slots, ns, length, model), jnp.bfloat16),
+            pltpu.VMEM((2, feat, LANES), jnp.bfloat16),
+            pltpu.VMEM((2, model, LANES), jnp.bfloat16),
+            pltpu.VMEM((max(1, inner - 1), outer) + block, f32),
+            pltpu.VMEM((max(1, inner - 1), outer) + block, f32),
+            pltpu.VMEM((outer,) + block, f32),
+            pltpu.VMEM((max(1, outer - 1),) + block, f32),
+            pltpu.VMEM((devices, ns * 8 + 8, LANES), f32),
+            many(slots, 4),
+            many(inner - 1, outer), many(inner - 1, outer),
+            many(outer - 1), many(outer - 1),
+            many(outer - 1), many(outer - 1),
+            many(inner - 1, outer), many(inner - 1, outer),
+            many(chips - 1), many(chips - 1),
+            many(chips), many(chips),
+            many(3),
+        ],
+        compiler_params=pltpu.CompilerParams(
+            collective_id=0, has_side_effects=True, vmem_limit_bytes=56 * 2**20
+        ),
+    )(tacts, tgrads, qacts, qgrads, pin, pout, tcount, qcount)
 
 
 def bcast_row(tile, i):
@@ -123,30 +354,18 @@
 def local(
     train_acts, train_grads, query_acts, query_grads, proj_in, proj_out, train_counts, query_counts
 ):
-    width = proj_in.shape[1]
-    length = train_acts.shape[1]
-    train_pair = project_pair(train_acts, train_grads, proj_in, proj_out)
-    query_pair = lax.psum(project_pair(query_acts, query_grads, proj_in, proj_out), "tensor")
-    query_sketch = form_sketches(query_pair, query_counts, width, length)
-    every_query = lax.all_gather(query_sketch, "dp", axis=0, tiled=True)
-    full_pair = lax.psum(train_pair, "tensor")
-    local_train = form_sketches(full_pair, train_counts, width, length)
-    every_train, every_count = (
-        lax.all_gather(local_train, "dp", axis=0, tiled=True),
-        lax.all_gather(train_counts, "dp", axis=0, tiled=True),
-    )
-    query_share = every_query.shape[0] // lax.axis_size("tensor")
-    my_queries = lax.dynamic_slice_in_dim(
-        every_query, lax.axis_index("tensor") * query_share, query_share
-    )
-    n = every_train.shape[0]
+    dps, tensor = lax.axis_size("dp"), lax.axis_size("tensor")
+    train, query, counts = sketches(
+        dps, tensor, train_acts, train_grads, query_acts, query_grads,
+        proj_in, proj_out, train_counts, query_counts,
+    )
     return solve(
-        every_train.reshape(-1, LANES),
-        my_queries.reshape(-1, LANES),
-        every_count.astype(jnp.float32).reshape(-1, LANES),
-        n,
-        query_share,
-        local_train.shape[0],
+        train.reshape(-1, LANES),
+        query.reshape(-1, LANES),
+        counts.reshape(-1, LANES),
+        train_acts.shape[0] * dps,
+        query_acts.shape[0] * dps // tensor,
+        train_acts.shape[0],
     )
 
 

time: 295 us -> 162 us (0.55)
  waiting for transfers between devices: 120 us -> 0 us
  Pallas kernels: 96.7 us -> 153 us
  matrix products: 42.4 us -> 0 us
  between operations: 14.2 us -> 0.02 us
  blocking collectives: 12.5 us -> 0 us
    psum x1 -> x0, waiting for transfers between devices: 119 us -> none  [local(): full_pair = lax.psum(train_pair, 'tensor')]
    pallas_call x0 -> x1, Pallas kernels: none -> 56.6 us  [sketches(): pl.pallas_call(functools.partial(sketch_kernel, dps, outer, inner), out_s...]
    dot_general x6 -> x0, matrix products: 42.4 us -> none  [the longest x2 29.1 us: project_pair(): jnp.einsum('stf,fr->srt', acts, proj_in, preferred_element_type=jnp.float32)]
    all_gather x1 -> x0, blocking collectives: 7.58 us -> none  [local(): every_query = lax.all_gather(query_sketch, 'dp', axis=0, tiled=True)]
    unnamed x15 -> x8, local copies, waits for them, and re-layouts: 0.89 us -> 6.8 us
    unnamed x1 -> x0, blocking collectives: 4.88 us -> none
    reshape x4 -> x0, local copies, waits for them, and re-layouts: 3.48 us -> none  [the longest x2 2.08 us: form_sketches(): return block.reshape(block.shape[0], width * width)]
  transfers between devices with their start and end apart: 2 -> 0, of which waited for: 2 -> 0; matrix products, arithmetic and copies ran while one was open for 1% -> 0% of each run, Pallas kernels for 0% -> 0%
where the time goes in v1:
time: 162 us; the launch traced here: 160 us
  Pallas kernels  153 us (94%)
  local copies, waits for them, and re-layouts  6.8 us (4%)
    pallas_call x1, Pallas kernels, solve(): pl.pallas_call(functools.partial(solve_kernel, rows_out, n), out_shape=ja...  96.7 us
    pallas_call x1, Pallas kernels, sketches(): pl.pallas_call(functools.partial(sketch_kernel, dps, outer, inner), out_s...  56.6 us
    unnamed x8, local copies, waits for them, and re-layouts  6.8 us

profile of v1, /device:TPU:0, one launch (start us, length us, event | category | flops | bytes accessed | tf_op | source)
XLA Modules:
  0.0 160.1 jit_solution(6459204217115148680)
XLA Ops:
  0.0 1.7 %copy.10.pout = bf16[1024,32]{1,0:T(8,128)(2,1)} copy(bf16[1024,32]{0,1:T(8,128)(2,1)} %param.13) | data formatting | bytes 131072 | tf_op args[5]
  1.7 2.2 %copy.9.pin = bf16[3584,32]{1,0:T(8,128)(2,1)} copy(bf16[3584,32]{0,1:T(8,128)(2,1)} %param.12) | data formatting | bytes 458752 | tf_op args[4]
  3.9 56.6 %shard_map.82 = (f32[32,64,128]{2,1,0:T(8,128)}, f32[4,16,128]{2,1,0:T(8,128)}, f32[32,8,128]{2,1,0:T(8,128)}) custom-call(bf16[64,64,3584]{2,1,0:T(8,128)(2,1)} %tacts.1, bf16[64,64,1024]{2,1,0:T(8,128)(2,1)} %tgrads.1, bf16[16,64,3584]{2,1,0:T(8,128)(2,1)} %qacts.1, bf16[16,64,1024]{2,1,0:T(8,128)(2,1)} %qgrads.1, bf16[3584,32]{1,0:T(8,128)(2,1)} %copy.9.pin, ...), custom_call_target="tpu_custom_call" | custom-call | tf_op jit(solution)/shard_map/pallas_call | solution.py:232
  60.6 0.0 copy-start
  60.6 1.2 copy-done
  61.8 0.0 copy-start.1
  61.8 0.9 copy-done.1
  62.7 0.0 copy-start.2
  62.7 0.8 copy-done.2
  63.5 96.7 %shard_map.83 = f32[8,64]{1,0:T(8,128)} custom-call(f32[2048,128]{1,0:T(8,128)S(1)} %bitcast.3, f32[64,128]{1,0:T(8,128)S(1)} %bitcast.5, f32[256,128]{1,0:T(8,128)S(1)} %bitcast.4), custom_call_target="tpu_custom_call" | custom-call | tf_op jit(solution)/shard_map/pallas_call | solution.py:340
Async XLA Ops:
  60.6 1.2 copy-start
  61.8 0.9 copy-start.1
  62.7 0.8 copy-start.2

commit v2 on v1

--- a/solution.py
+++ b/solution.py
@@ -8,6 +8,7 @@
 from jax.sharding import PartitionSpec as P
 
 LANES = 128
+PANEL = 32
 
 
 def place(width, offset):
@@ -271,7 +272,7 @@
     return jnp.take_along_axis(tile, index, axis=1, mode="promise_in_bounds")
 
 
-def solve_kernel(rows_out, scale, s_ref, q_ref, cnt_ref, out_ref, wide, qwide, a_ref):
+def solve_kernel(rows_out, scale, s_ref, q_ref, cnt_ref, out_ref, wide, qwide, a_ref, panel, wpad):
     n = a_ref.shape[0]
     nq = qwide.shape[0]
     parts = s_ref.shape[0] // n
@@ -291,46 +292,61 @@
     sub = lax.broadcasted_iota(jnp.int32, (8, LANES), 0)
     lane = lax.broadcasted_iota(jnp.int32, (8, LANES), 1)
 
+    wpad[...] = jnp.zeros_like(wpad)
+    full_lane = lax.broadcasted_iota(jnp.int32, (n, n), 1)
+    tile_lane = lax.broadcasted_iota(jnp.int32, (n, LANES), 1)
+
     def block(kb, carry):
-        k0 = pl.multiple_of(kb * 8, 8)
-        kt = pl.multiple_of((k0 // LANES) * LANES, LANES)
-        kl = k0 % LANES
-        picks = [jnp.full((8, LANES), kl + i, jnp.int32) for i in range(8)]
-        pivot = a_ref[pl.ds(k0, 8), pl.ds(kt, LANES)]
-        cols = [lane_pick(pivot, picks[i]) for i in range(8)]
-        inside, right = [], []
-        for j in range(tiles):
-            offset = lane + (j * LANES - k0)
-            mask = (offset >= 0) & (offset < 8)
-            inside.append(mask)
-            row = a_ref[pl.ds(k0, 8), j * LANES : (j + 1) * LANES]
-            right.append(jnp.where(mask, jnp.where(offset == sub, 1.0, 0.0), row))
-        for i in range(8):
-            own = sub == i
-            inv = 1.0 / bcast_row(cols[i], i)
-            factor = cols[i]
-            for m in range(i + 1, 8):
-                row = bcast_row(cols[m], i) * inv
-                cols[m] = jnp.where(own, row, cols[m] - factor * row)
+        base = pl.multiple_of(kb * PANEL, PANEL)
+        kt = pl.multiple_of((base // LANES) * LANES, LANES)
+        kl = pl.multiple_of(base % LANES, PANEL)
+        panel[...] = a_ref[pl.ds(base, PANEL), :]
+        for sb in range(PANEL // 8):
+            k0 = base + sb * 8
+            mine = slice(sb * 8, sb * 8 + 8)
+            picks = [jnp.full((8, LANES), kl + sb * 8 + i, jnp.int32) for i in range(8)]
+            pivot = panel[mine, pl.ds(kt, LANES)]
+            cols = [lane_pick(pivot, picks[i]) for i in range(8)]
+            inside, right = [], []
             for j in range(tiles):
-                row = bcast_row(right[j], i) * inv
-                right[j] = jnp.where(own, row, right[j] - factor * row)
-        spread = [[bcast_row(right[j], i) for j in range(tiles)] for i in range(8)]
-        for rt in range(n // 8):
-            here = slice(rt * 8, rt * 8 + 8)
-            column = a_ref[here, pl.ds(kt, LANES)]
-            heads = [lane_pick(column, picks[i]) for i in range(8)]
+                offset = lane + (j * LANES - k0)
+                mask = (offset >= 0) & (offset < 8)
+                inside.append(mask)
+                row = panel[mine, j * LANES : (j + 1) * LANES]
+                right.append(jnp.where(mask, jnp.where(offset == sub, 1.0, 0.0), row))
+            for i in range(8):
+                here = sub == i
+                inv = 1.0 / bcast_row(cols[i], i)
+                factor = cols[i]
+                for m in range(i + 1, 8):
+                    row = bcast_row(cols[m], i) * inv
+                    cols[m] = jnp.where(here, row, cols[m] - factor * row)
+                for j in range(tiles):
+                    row = bcast_row(right[j], i) * inv
+                    right[j] = jnp.where(here, row, right[j] - factor * row)
+            for rt in range(PANEL // 8):
+                if rt == sb:
+                    continue
+                here = slice(rt * 8, rt * 8 + 8)
+                column = panel[here, pl.ds(kt, LANES)]
+                heads = [lane_pick(column, picks[i]) for i in range(8)]
+                for j in range(tiles):
+                    there = slice(j * LANES, (j + 1) * LANES)
+                    value = jnp.where(inside[j], 0.0, panel[here, there])
+                    for i in range(8):
+                        value = value - heads[i] * bcast_row(right[j], i)
+                    panel[here, there] = value
             for j in range(tiles):
-                there = slice(j * LANES, (j + 1) * LANES)
-                value = jnp.where(inside[j], 0.0, a_ref[here, there])
-                for i in range(8):
-                    value = value - heads[i] * spread[i][j]
-                a_ref[here, there] = value
-        for j in range(tiles):
-            a_ref[pl.ds(k0, 8), j * LANES : (j + 1) * LANES] = right[j]
+                panel[mine, j * LANES : (j + 1) * LANES] = right[j]
+        wpad[pl.ds(kl, PANEL), :] = panel[...]
+        near = (tile_lane >= kl) & (tile_lane < kl + PANEL)
+        column = jnp.where(near, a_ref[:, pl.ds(kt, LANES)], 0.0)
+        drop = (full_lane >= base) & (full_lane < base + PANEL)
+        a_ref[...] = jnp.where(drop, 0.0, a_ref[...]) - jnp.dot(column, wpad[...], **exact)
+        a_ref[pl.ds(base, PANEL), :] = panel[...]
         return carry
 
-    lax.fori_loop(0, n // 8, block, 0)
+    lax.fori_loop(0, n // PANEL, block, 0)
     first = pl.multiple_of(lax.axis_index("dp") * rows_out, 8)
     out_ref[...] = lax.dot_general(cross, a_ref[pl.ds(first, rows_out), :], dims, **exact) / scale
 
@@ -346,6 +362,8 @@
             pltpu.VMEM((n, width), jnp.float32),
             pltpu.VMEM((nq, width), jnp.float32),
             pltpu.VMEM((n, n), jnp.float32),
+            pltpu.VMEM((PANEL, n), jnp.float32),
+            pltpu.VMEM((LANES, n), jnp.float32),
         ],
         compiler_params=pltpu.CompilerParams(vmem_limit_bytes=48 * 2**20),
     )(train, query, counts)

time: 162 us -> 81.6 us (0.50)
  Pallas kernels: 153 us -> 73.4 us
    pallas_call x1, Pallas kernels: 96.7 us -> 16.8 us  [solve(): pl.pallas_call(functools.partial(solve_kernel, rows_out, n), out_shape=ja...]
where the time goes in v2:
time: 81.6 us; the launch traced here: 80.2 us
  Pallas kernels  73.4 us (90%)
  local copies, waits for them, and re-layouts  6.8 us (8%)
    pallas_call x1, Pallas kernels, sketches(): pl.pallas_call(functools.partial(sketch_kernel, dps, outer, inner), out_s...  56.6 us
    pallas_call x1, Pallas kernels, solve(): pl.pallas_call(functools.partial(solve_kernel, rows_out, n), out_shape=ja...  16.8 us
    unnamed x8, local copies, waits for them, and re-layouts  6.8 us

profile of v2, /device:TPU:0, one launch (start us, length us, event | category | flops | bytes accessed | tf_op | source)
XLA Modules:
  0.0 80.2 jit_solution(9742373956904089834)
XLA Ops:
  0.0 1.7 %copy.10.pout = bf16[1024,32]{1,0:T(8,128)(2,1)} copy(bf16[1024,32]{0,1:T(8,128)(2,1)} %param.13) | data formatting | bytes 131072 | tf_op args[5]
  1.7 2.2 %copy.9.pin = bf16[3584,32]{1,0:T(8,128)(2,1)} copy(bf16[3584,32]{0,1:T(8,128)(2,1)} %param.12) | data formatting | bytes 458752 | tf_op args[4]
  3.9 56.6 %shard_map.82 = (f32[32,64,128]{2,1,0:T(8,128)}, f32[4,16,128]{2,1,0:T(8,128)}, f32[32,8,128]{2,1,0:T(8,128)}) custom-call(bf16[64,64,3584]{2,1,0:T(8,128)(2,1)} %tacts.1, bf16[64,64,1024]{2,1,0:T(8,128)(2,1)} %tgrads.1, bf16[16,64,3584]{2,1,0:T(8,128)(2,1)} %qacts.1, bf16[16,64,1024]{2,1,0:T(8,128)(2,1)} %qgrads.1, bf16[3584,32]{1,0:T(8,128)(2,1)} %copy.9.pin, ...), custom_call_target="tpu_custom_call" | custom-call | tf_op jit(solution)/shard_map/pallas_call | solution.py:233
  60.6 0.0 copy-start
  60.6 1.2 %copy-done = f32[32,64,128]{2,1,0:T(8,128)S(1)} copy-done((f32[32,64,128]{2,1,0:T(8,128)S(1)}, f32[32,64,128]{2,1,0:T(8,128)}, u32[]{:S(2)}) %copy-start) | copy-done | bytes 1048600
  61.8 0.0 copy-start.1
  61.8 0.9 %copy-done.1 = f32[32,8,128]{2,1,0:T(8,128)S(1)} copy-done((f32[32,8,128]{2,1,0:T(8,128)S(1)}, f32[32,8,128]{2,1,0:T(8,128)}, u32[]{:S(2)}) %copy-start.1) | copy-done | bytes 131096
  62.7 0.0 copy-start.2
  62.7 0.8 copy-done.2
  63.5 16.8 %shard_map.83 = f32[8,64]{1,0:T(8,128)} custom-call(f32[2048,128]{1,0:T(8,128)S(1)} %bitcast.3, f32[64,128]{1,0:T(8,128)S(1)} %bitcast.5, f32[256,128]{1,0:T(8,128)S(1)} %bitcast.4), custom_call_target="tpu_custom_call" | custom-call | tf_op jit(solution)/shard_map/pallas_call | solution.py:356
Async XLA Ops:
  60.6 1.2 %copy-start = (f32[32,64,128]{2,1,0:T(8,128)S(1)}, f32[32,64,128]{2,1,0:T(8,128)}, u32[]{:S(2)}) copy-start(f32[32,64,128]{2,1,0:T(8,128)} %get-tuple-element.8) | copy-start | bytes 3145732
  61.8 0.9 %copy-start.1 = (f32[32,8,128]{2,1,0:T(8,128)S(1)}, f32[32,8,128]{2,1,0:T(8,128)}, u32[]{:S(2)}) copy-start(f32[32,8,128]{2,1,0:T(8,128)} %get-tuple-element.10) | copy-start | bytes 393220
  62.7 0.8 copy-start.2

commit v3 on v2

--- a/solution.py
+++ b/solution.py
@@ -24,12 +24,12 @@
     abuf, gbuf, win, wout, yout, yin, own, zin, gath,
     load_sem, ysend, yrecv, zsend, zrecv, gzs, gzr, gys, gyr, gxs, gxr, gcs, gcr, out_sem,
 ):
-    width = pin.shape[1]
+    width = pin.shape[0]
     tensor = outer * inner
     nt, nq = tacts.shape[0] // tensor, qacts.shape[0] // tensor
     ns = nt + nq
     half = tacts.shape[1] // 2
-    feat, model = pin.shape[0], pout.shape[0]
+    feat, model = pin.shape[1], pout.shape[1]
     chips = dps // 2
     dp, me = lax.axis_index("dp"), lax.axis_index("tensor")
     z, y = me // inner, me % inner
@@ -76,11 +76,13 @@
         pl.semaphore_signal(barrier, inc=1, device_id=partner, device_id_type=mesh_id)
 
     for h in range(2):
-        win[h] = jnp.dot(
-            pin[...], place(width, 2 * width * h + width), preferred_element_type=jnp.float32
+        win[h] = lax.dot_general(
+            pin[...], place(width, 2 * width * h + width), (((0,), (0,)), ((), ())),
+            preferred_element_type=jnp.float32,
         ).astype(jnp.bfloat16)
-        wout[h] = jnp.dot(
-            pout[...], place(width, 2 * width * h), preferred_element_type=jnp.float32
+        wout[h] = lax.dot_general(
+            pout[...], place(width, 2 * width * h), (((0,), (0,)), ((), ())),
+            preferred_element_type=jnp.float32,
         ).astype(jnp.bfloat16)
     pl.semaphore_wait(barrier, len(partners))
 
@@ -182,23 +184,34 @@
         return copy
 
     zs = [share(gath.at[mine], gzs.at[k - 1], gzr.at[k - 1], at_z(k)) for k in range(1, outer)]
-    ys = []
+    ys, xs = {}, {}
+
+    def share_x(j, k):
+        slot = ((z - j + outer) % outer) * inner + (y - k + inner) % inner
+        block = gath.at[dp * tensor + slot]
+        order = j * inner + k
+        for c in range(1, chips):
+            xs[c, j, k] = share(block, gxs.at[c - 1, order], gxr.at[c - 1, order], at_x(c))
+
     for j in range(outer):
         if j:
             zs[j - 1].wait_recv()
         block = gath.at[dp * tensor + ((z - j + outer) % outer) * inner + y]
         for k in range(1, inner):
-            ys.append(share(block, gys.at[k - 1, j], gyr.at[k - 1, j], at_y(k)))
-    for copy in ys:
-        copy.wait_recv()
-    block = gath.at[pl.ds(dp * tensor, tensor)]
-    xs = [share(block, gxs.at[k - 1], gxr.at[k - 1], at_x(k)) for k in range(1, chips)]
+            ys[j, k] = share(block, gys.at[k - 1, j], gyr.at[k - 1, j], at_y(k))
+        share_x(j, 0)
+    for j in range(outer):
+        for k in range(1, inner):
+            ys[j, k].wait_recv()
+            share_x(j, k)
     cs = []
-    for j in range(chips):
-        if j:
-            xs[j - 1].wait_recv()
-        block = gath.at[pl.ds((((x - j + chips) % chips) * 2 + core) * tensor, tensor)]
-        cs.append(share(block, gcs.at[j], gcr.at[j], sibling))
+    for c in range(chips):
+        if c:
+            for j in range(outer):
+                for k in range(inner):
+                    xs[c, j, k].wait_recv()
+        block = gath.at[pl.ds((((x - c + chips) % chips) * 2 + core) * tensor, tensor)]
+        cs.append(share(block, gcs.at[c], gcr.at[c], sibling))
     for copy in cs:
         copy.wait_recv()
     finals = [
@@ -254,7 +267,7 @@
             many(outer - 1), many(outer - 1),
             many(outer - 1), many(outer - 1),
             many(inner - 1, outer), many(inner - 1, outer),
-            many(chips - 1), many(chips - 1),
+            many(chips - 1, tensor), many(chips - 1, tensor),
             many(chips), many(chips),
             many(3),
         ],
@@ -375,7 +388,7 @@
     dps, tensor = lax.axis_size("dp"), lax.axis_size("tensor")
     train, query, counts = sketches(
         dps, tensor, train_acts, train_grads, query_acts, query_grads,
-        proj_in, proj_out, train_counts, query_counts,
+        proj_in.T, proj_out.T, train_counts, query_counts,
     )
     return solve(
         train.reshape(-1, LANES),

time: 81.6 us -> 73.7 us (0.903)
  local copies, waits for them, and re-layouts: 6.8 us -> 2.88 us
  Pallas kernels: 73.4 us -> 69.7 us
    unnamed x8 -> x6, local copies, waits for them, and re-layouts: 6.8 us -> 2.88 us
    pallas_call x1, Pallas kernels: 56.6 us -> 52.9 us  [sketches(): pl.pallas_call(functools.partial(sketch_kernel, dps, outer, inner), out_s...]
where the time goes in v3:
time: 73.7 us; the launch traced here: 72.6 us
  Pallas kernels  69.7 us (95%)
  local copies, waits for them, and re-layouts  2.88 us (4%)
    pallas_call x1, Pallas kernels, sketches(): pl.pallas_call(functools.partial(sketch_kernel, dps, outer, inner), out_s...  52.9 us
    pallas_call x1, Pallas kernels, solve(): pl.pallas_call(functools.partial(solve_kernel, rows_out, n), out_shape=ja...  16.8 us
    unnamed x6, local copies, waits for them, and re-layouts  2.88 us

profile of v3, /device:TPU:0, one launch (start us, length us, event | category | flops | bytes accessed | tf_op | source)
XLA Modules:
  0.0 72.6 jit_solution(16320397484890942540)
XLA Ops:
  0.0 52.9 %shard_map.82 = (f32[32,64,128]{2,1,0:T(8,128)}, f32[4,16,128]{2,1,0:T(8,128)}, f32[32,8,128]{2,1,0:T(8,128)}) custom-call(bf16[64,64,3584]{2,1,0:T(8,128)(2,1)} %tacts.1, bf16[64,64,1024]{2,1,0:T(8,128)(2,1)} %tgrads.1, bf16[16,64,3584]{2,1,0:T(8,128)(2,1)} %qacts.1, bf16[16,64,1024]{2,1,0:T(8,128)(2,1)} %qgrads.1, bf16[32,3584]{1,0:T(8,128)(2,1)} %bitcast.8, ...), custom_call_target="tpu_custom_call" | custom-call | tf_op jit(solution)/shard_map/pallas_call | solution.py:246
  52.9 0.0 copy-start
  52.9 1.2 %copy-done = f32[32,64,128]{2,1,0:T(8,128)S(1)} copy-done((f32[32,64,128]{2,1,0:T(8,128)S(1)}, f32[32,64,128]{2,1,0:T(8,128)}, u32[]{:S(2)}) %copy-start) | copy-done | bytes 1048600
  54.1 0.0 copy-start.1
  54.1 0.9 %copy-done.1 = f32[32,8,128]{2,1,0:T(8,128)S(1)} copy-done((f32[32,8,128]{2,1,0:T(8,128)S(1)}, f32[32,8,128]{2,1,0:T(8,128)}, u32[]{:S(2)}) %copy-start.1) | copy-done | bytes 131096
  55.0 0.0 copy-start.2
  55.0 0.8 %copy-done.2 = f32[4,16,128]{2,1,0:T(8,128)S(1)} copy-done((f32[4,16,128]{2,1,0:T(8,128)S(1)}, f32[4,16,128]{2,1,0:T(8,128)}, u32[]{:S(2)}) %copy-start.2) | copy-done | bytes 32792
  55.8 16.8 %shard_map.83 = f32[8,64]{1,0:T(8,128)} custom-call(f32[2048,128]{1,0:T(8,128)S(1)} %bitcast.5, f32[64,128]{1,0:T(8,128)S(1)} %bitcast.7, f32[256,128]{1,0:T(8,128)S(1)} %bitcast.6), custom_call_target="tpu_custom_call" | custom-call | tf_op jit(solution)/shard_map/pallas_call | solution.py:369
Async XLA Ops:
  52.9 1.2 %copy-start = (f32[32,64,128]{2,1,0:T(8,128)S(1)}, f32[32,64,128]{2,1,0:T(8,128)}, u32[]{:S(2)}) copy-start(f32[32,64,128]{2,1,0:T(8,128)} %get-tuple-element.8) | copy-start | bytes 3145732
  54.1 0.9 %copy-start.1 = (f32[32,8,128]{2,1,0:T(8,128)S(1)}, f32[32,8,128]{2,1,0:T(8,128)}, u32[]{:S(2)}) copy-start(f32[32,8,128]{2,1,0:T(8,128)} %get-tuple-element.10) | copy-start | bytes 393220
  55.0 0.8 %copy-start.2 = (f32[4,16,128]{2,1,0:T(8,128)S(1)}, f32[4,16,128]{2,1,0:T(8,128)}, u32[]{:S(2)}) copy-start(f32[4,16,128]{2,1,0:T(8,128)} %get-tuple-element.9) | copy-start | bytes 98308
